TPU v7x, 128 devices: a whole 4x4x4 slice. The times are simulated.
128 devices in a mesh: gx: 16 (over x, z), gy: 8 (over y, core).
Axes of the slice: x: 4, y: 4, z: 4, core: 2. Of those that a mesh axis runs over, the one named last changes fastest.
Arguments:
- features: bfloat16 [128, 32, 32, 256], P(None, 'gx', 'gy'), may hold values from -6 to 6
- labels: int32 [32, 32, 256], P('gx', 'gy'), may hold values from 0 to 3
- w_down: bfloat16 [2, 2, 2, 256, 128], replicated, may hold values from -0.1875 to 0.1875
- w_mid: bfloat16 [3, 3, 3, 256, 256], replicated, may hold values from -0.078125 to 0.078125
- w_up: bfloat16 [4, 4, 4, 128, 256], replicated, may hold values from -0.125 to 0.125
- w_head: bfloat16 [4, 128], replicated, may hold values from -0.5 to 0.5
Outputs:
- feature_grad: bfloat16 [128, 32, 32, 256], P(None, 'gx', 'gy')
- mid_weight_grad: bfloat16 [3, 3, 3, 256, 256], replicated
- up_weight_grad: bfloat16 [4, 4, 4, 128, 256], replicated
All inputs are finite; a program needn't handle non-finite values.
Results may differ from a plain program's by a relative error of at most 0.0085.
Values may be sent and summed in bfloat16 or wider, within the bound.
A program may use at most 128 MiB of HBM per device.

v0:
```python
import functools
import math

import jax
import jax.numpy as jnp
from jax import lax
from jax.experimental import pallas as pl
from jax.experimental.pallas import tpu as pltpu
from jax.sharding import PartitionSpec as P

MESH = pl.DeviceIdType.MESH
ROWS = 7680
PART = ROWS // 3
SIZES = [(640, 320), (160, 80), (48, 32)]
THIRD = 4 * 48
STEP = 80


def my_place():
    gx, gy = lax.axis_index("gx"), lax.axis_index("gy")
    return lax.div(gx, 4), lax.div(gy, 2), lax.rem(gx, 4), lax.rem(gy, 2)


def device_at(x, y, z, core):
    return (x * 4 + z, y * 2 + core)


def moved(place, axis, distance):
    spot = list(place)
    spot[axis] = lax.rem(spot[axis] + distance, 4)
    return device_at(*spot)


def rows_at(start, count):
    return pl.ds(pl.multiple_of(start, 16), count)


def for_rows(count, step, body):
    def one(i, carry):
        body(i * step)
        return carry

    lax.fori_loop(0, count // step, one, 0)


class Summing:
    axes = [(0, 1, 2), (1, 2, 0), (2, 0, 1)]

    def __init__(self, part, out, got, work, half, slabs, sums, piece, res, send_sem, recv_sem):
        self.part, self.out, self.got, self.work, self.half = part, out, got, work, half
        self.slabs, self.sums, self.piece, self.res = slabs, sums, piece, res
        self.send_sem, self.recv_sem = send_sem, recv_sem
        self.place = my_place()
        self.core = self.place[3]
        self.other = device_at(*self.place[:3], 1 - self.core)
        self.count, self.sent, self.outs = 0, [], []
        self.first, self.opened, self.spread = {}, {}, {}

    def peers(self):
        places = [moved(self.place, axis, d) for axis in range(3) for d in (1, 2, 3)]
        return [self.other] + places

    def send(self, src, dst, target):
        copy = pltpu.make_async_remote_copy(
            src_ref=src, dst_ref=dst, send_sem=self.send_sem.at[self.count],
            recv_sem=self.recv_sem.at[self.count], device_id=target, device_id_type=MESH,
        )
        self.count += 1
        copy.start()
        self.sent.append(copy)
        return copy

    def spots(self, k, level):
        p = self.place[self.axes[k][level]]
        return p, lax.rem(p + 1, 4), lax.rem(p + 2, 4), lax.rem(p + 3, 4)

    def peer(self, k, level, distance):
        return moved(self.place, self.axes[k][level], distance)

    def send_other(self, k):
        rows = pl.ds(k * PART, PART)
        src = self.part.at[1 - self.core, rows]
        self.first[k] = self.send(src, self.got.at[rows], self.other)

    def add_other(self, k):
        self.first[k].wait_recv()

        def body(start):
            rows = rows_at(k * PART + start, STEP)
            self.work[rows] = self.part[self.core, rows] + self.got[rows]

        for_rows(PART, STEP, body)

    def open_ring(self, k):
        size, cut = SIZES[0]
        _, up, far, down = self.spots(k, 0)
        after, before = self.peer(k, 0, 1), self.peer(k, 0, 3)
        base = k * PART
        src, slab = self.work, self.slabs[0]
        self.opened[k, 0] = [
            self.send(src.at[rows_at(base + far * size, cut)], self.half.at[k, 0], after),
            self.send(src.at[rows_at(base + far * size + cut, cut)], self.half.at[k, 1], before),
            self.send(src.at[rows_at(base + up * size + cut, cut)],
                      slab.at[k, 0, pl.ds(cut, cut)], after),
            self.send(src.at[rows_at(base + down * size, cut)], slab.at[k, 1, pl.ds(0, cut)],
                      before),
        ]

    def pass_ring(self, k):
        size, cut = SIZES[0]
        _, up, _, down = self.spots(k, 0)
        base = k * PART
        slab, copies = self.slabs[0], self.opened[k, 0]
        for side, start, target, at in (
            (0, base + up * size, self.peer(k, 0, 1), 0),
            (1, base + down * size + cut, self.peer(k, 0, 3), cut),
        ):
            copies[side].wait_recv()

            def body(offset):
                rows = rows_at(start + offset, STEP)
                passed = self.half[k, side, rows_at(offset, STEP)]
                self.work[rows] = self.work[rows] + passed

            for_rows(cut, STEP, body)
            copies.append(
                self.send(self.work.at[rows_at(start, cut)], slab.at[k, side, pl.ds(at, cut)],
                          target)
            )

    def open_level(self, k, level):
        size = SIZES[level][0]
        src, base = self.sums[level - 1], k * 4 * size
        spots = self.spots(k, level)
        self.opened[k, level] = [
            self.send(src.at[rows_at(base + spots[d] * size, size)],
                      self.slabs[level].at[k, d - 1], self.peer(k, level, d))
            for d in (1, 2, 3)
        ]

    def close_level(self, k, level, store):
        size = SIZES[level][0]
        step = 48 if level == 2 else STEP
        copies = self.opened[k, level]
        for copy in copies[2:] if level == 0 else copies:
            copy.wait_recv()
        src, base = (self.work, k * PART) if level == 0 else (self.sums[level - 1], k * 4 * size)
        base = base + self.spots(k, level)[0] * size
        slab = self.slabs[level]

        def body(start):
            total = src[rows_at(base + start, step)].astype(jnp.float32)
            for side in range(slab.shape[1]):
                total = total + slab[k, side, rows_at(start, step)].astype(jnp.float32)
            store(start, total)

        for_rows(size, step, body)

    def store_sum(self, k, level):
        pitch = PART // 4 if level == 0 else THIRD

        def store(start, total):
            self.sums[level][rows_at(k * pitch + start, STEP)] = total.astype(jnp.bfloat16)

        self.close_level(k, level, store)
        if level == 1:
            self.sums[1][pl.ds(k * THIRD + 160, 32)] = jnp.zeros((32, 128), jnp.bfloat16)

    def store_last(self, k, scale):
        def store(start, total):
            rows = rows_at(k * THIRD + self.spots(k, 2)[0] * 48 + start, 48)
            self.piece[rows] = (total * scale).astype(jnp.bfloat16)

        self.close_level(k, 2, store)

    def spread_rows(self, k, level):
        if level == 2:
            return self.piece, k * THIRD
        base = k * PART
        if level == 1:
            base = base + self.spots(k, 0)[0] * SIZES[0][0]
        return self.res, base

    def open_spread(self, k, level):
        size = SIZES[level][0]
        ref, base = self.spread_rows(k, level)
        rows = rows_at(base + self.spots(k, level)[0] * size, size)
        self.spread[k, level] = [
            self.send(ref.at[rows], ref.at[rows], self.peer(k, level, d))
            for d in ((1, 3) if level == 0 else (1, 2, 3))
        ]

    def close_spread(self, k, level):
        for copy in self.spread[k, level]:
            copy.wait_recv()
        if level == 2:
            base = k * PART + self.spots(k, 0)[0] * 640 + self.spots(k, 1)[0] * 160
            self.res[rows_at(base, 160)] = self.piece[pl.ds(k * THIRD, 160)]

    def hand_out(self, start, count):
        rows = rows_at(start, count)
        lanes = pl.ds(pl.multiple_of(self.core * 128, 128), 128)
        near = pltpu.make_async_copy(
            self.res.at[rows], self.out.at[rows, lanes], self.send_sem.at[self.count]
        )
        self.count += 1
        near.start()
        self.outs.append((near, self.send(self.res.at[rows], self.out.at[rows, lanes], self.other)))

    def hand_own(self, k):
        self.hand_out(k * PART + self.spots(k, 0)[0] * 640, 640)

    def pass_spread(self, k):
        size, cut = SIZES[0]
        base = k * PART
        _, up, far, down = self.spots(k, 0)
        copies = self.spread[k, 0]
        copies[0].wait_recv()
        rows = rows_at(base + down * size, cut)
        copies.append(self.send(self.res.at[rows], self.res.at[rows], self.peer(k, 0, 1)))
        copies[1].wait_recv()
        rows = rows_at(base + up * size + cut, cut)
        copies.append(self.send(self.res.at[rows], self.res.at[rows], self.peer(k, 0, 3)))

    def hand_sides(self, k):
        _, up, _, down = self.spots(k, 0)
        self.hand_out(k * PART + down * 640, 640)
        self.hand_out(k * PART + up * 640, 640)

    def hand_far(self, k):
        for copy in self.spread[k, 0][2:]:
            copy.wait_recv()
        self.hand_out(k * PART + self.spots(k, 0)[2] * 640, 640)

    def end(self):
        for copy in self.sent:
            copy.wait_send()
        for near, far in self.outs:
            near.wait()
            far.wait_recv()


NEAR = [(0, 1), (0, -1), (1, 0), (-1, 0), (1, 1), (1, -1), (-1, 1), (-1, -1)]
NN = (((1,), (0,)), ((), ()))
NT = (((1,), (1,)), ((), ()))
TN = (((0,), (0,)), ((), ()))


def dot(left, right, dims=NN):
    return lax.dot_general(left, right, dims, preferred_element_type=jnp.float32)


def silu(value):
    return value * jax.nn.sigmoid(value)


def silu_slope(value):
    gate = jax.nn.sigmoid(value)
    return gate * (1.0 + value * (1.0 - gate))


def grid_of(rows, cols):
    return (
        lax.broadcasted_iota(jnp.int32, (rows, cols), 0),
        lax.broadcasted_iota(jnp.int32, (rows, cols), 1),
    )


def table(mask):
    return mask.astype(jnp.float32).astype(jnp.bfloat16)


def later_cell(block):
    lane = lax.broadcasted_iota(jnp.int32, block.shape, 1)
    return jnp.where(lane == 127, 0.0, pltpu.roll(block, 127, 1))


def earlier_cell(block):
    lane = lax.broadcasted_iota(jnp.int32, block.shape, 1)
    return jnp.where(lane == 0, 0.0, pltpu.roll(block, 1, 1))


def window_kernel(scale, features, labels, w_down, head_rows, w_mid_hbm, w_up_hbm, grad_out, sum_out,
                  w_head, label_cells, w_mid, w_up, low, low_moved, down_pre, mid_pre, split, head, head_t,
                  partial, arrived, logit_grad, columns, back, back_moved,
                  part, got, work, half, slab0, slab1, slab2, sum0, sum1, piece, res,
                  load_sem, send_sem, recv_sem, sum_send, sum_recv):
    gx, gy = lax.axis_index("gx"), lax.axis_index("gy")

    def near(dx, dy):
        return (lax.rem(gx + (dx + 16), 16), lax.rem(gy + (dy + 8), 8))

    loads = [
        pltpu.make_async_copy(w_mid_hbm, w_mid, load_sem.at[0]),
        pltpu.make_async_copy(w_up_hbm, w_up, load_sem.at[1]),
    ]
    for load in loads:
        load.start()
    barrier = pltpu.get_barrier_semaphore()
    summing = Summing(
        part, sum_out, got, work, half, (slab0, slab1, slab2), (sum0, sum1), piece, res,
        sum_send, sum_recv,
    )
    peers = [near(dx, dy) for dx, dy in NEAR] + summing.peers()
    for peer in peers:
        pl.semaphore_signal(barrier, inc=1, device_id=peer, device_id_type=MESH)
    w_head[...] = jnp.zeros((16, 128), jnp.float32)
    w_head[pl.ds(0, 4), :] = head_rows[...].astype(jnp.float32)
    heads = w_head[...].astype(jnp.bfloat16)
    for a in (0, 1):
        label_cells[pl.ds(4 * a, 4), :] = labels[a].astype(jnp.float32)

    sent = []

    def exchange(stage, src, dst, places):
        copies = []
        for index, (dx, dy) in enumerate(NEAR):
            src_x, dst_x, src_y, dst_y = places(dx, dy)
            copy = pltpu.make_async_remote_copy(
                src_ref=src.at[src_x, src_y], dst_ref=dst.at[dst_x, dst_y],
                send_sem=send_sem.at[8 * stage + index], recv_sem=recv_sem.at[8 * stage + index],
                device_id=near(dx, dy), device_id_type=MESH,
            )
            copy.start()
            copies.append(copy)
        sent.extend(copies)
        return copies

    def finish(copies, buffer):
        for copy in copies:
            copy.wait_recv()
        wide, tall = buffer.shape[0], buffer.shape[1]

        @pl.when(gx == 0)
        def _():
            buffer[0] = jnp.zeros(buffer.shape[1:], buffer.dtype)

        @pl.when(gx == 15)
        def _():
            buffer[wide - 1] = jnp.zeros(buffer.shape[1:], buffer.dtype)

        @pl.when(gy == 0)
        def _():
            for x in range(wide):
                buffer[x, 0] = jnp.zeros(buffer.shape[2:], buffer.dtype)

        @pl.when(gy == 7)
        def _():
            for x in range(wide):
                buffer[x, tall - 1] = jnp.zeros(buffer.shape[2:], buffer.dtype)

    one = lambda i: pl.ds(i, 1)

    def brick_places(dx, dy):
        src_y = {0: pl.ds(1, 2), 1: one(2), -1: one(1)}[dy]
        dst_y = {0: pl.ds(1, 2), 1: one(0), -1: one(3)}[dy]
        return one(1), one(1 - dx), src_y, dst_y

    def upper_places(dx, dy):
        src_x = {0: pl.ds(1, 2), 1: one(2), -1: one(1)}[dx]
        dst_x = {0: pl.ds(1, 2), 1: one(0), -1: one(3)}[dx]
        src_y = {0: pl.ds(1, 4), 1: one(4), -1: one(1)}[dy]
        dst_y = {0: pl.ds(1, 4), 1: one(0), -1: one(5)}[dy]
        return src_x, dst_x, src_y, dst_y

    def spill_places(dx, dy):
        src_x = {0: pl.ds(1, 2), 1: one(3), -1: one(0)}[dx]
        src_y = {0: pl.ds(1, 4), 1: one(5), -1: one(0)}[dy]
        _, dst_x, _, dst_y = upper_places(dx, dy)
        return src_x, dst_x, src_y, dst_y

    lanes = lambda i: pl.ds(i * 128, 128)
    rows, cols = grid_of(256, 256)
    apart = table(rows == jnp.where(cols < 128, 2 * cols, 2 * cols - 255))
    split[...] = dot(features[...], apart).astype(jnp.bfloat16)
    total = jnp.zeros((256, 256), jnp.float32)
    for a in (0, 1):
        for b in (0, 1):
            weight = jnp.concatenate([w_down[4 * a + 2 * b], w_down[4 * a + 2 * b + 1]], axis=1)
            cells = [
                jnp.concatenate(
                    [split[pl.ds((4 * a + 2 * y + b) * 128, 128), lanes(c)] for y in (0, 1)],
                    axis=1,
                )
                for c in (0, 1)
            ]
            total = total + dot(weight, jnp.concatenate(cells, axis=0))
    down_pre[...] = total
    total = silu(total).astype(jnp.bfloat16)
    low[1, 1] = total[:, :128]
    low[1, 2] = total[:, 128:]
    pl.semaphore_wait(barrier, len(peers))
    copies = exchange(0, low, low, brick_places)

    label_rows = dot(label_cells[...].astype(jnp.bfloat16), apart)
    loads[1].wait()
    for tap in range(64):
        mixed = dot(heads, w_up[pl.ds(tap * 128, 128), :])
        head[pl.ds(tap * 8, 8), :] = mixed[:8]
    head_t[...] = jnp.transpose(head[...])
    loads[0].wait()

    finish(copies, low)
    rows, cols = grid_of(128, 256)
    moves = table(rows == jnp.where(cols < 128, cols - 1, cols - 127))
    for x in range(3):
        for y in range(4):
            low_moved[1, x, y] = low[x, y]
            both = dot(low[x, y], moves).astype(jnp.bfloat16)
            low_moved[0, x, y] = both[:, :128]
            low_moved[2, x, y] = both[:, 128:]
    total = jnp.zeros((256, 256), jnp.float32)
    for a in range(3):
        for b in range(3):
            taps = [9 * a + 3 * b + c for c in range(3)]
            weight = jnp.concatenate([w_mid[pl.ds(t * 256, 256), :] for t in taps], axis=1)
            cells = [
                jnp.concatenate([low_moved[c, a, b], low_moved[c, a, b + 1]], axis=1)
                for c in range(3)
            ]
            total = total + dot(weight, jnp.concatenate(cells, axis=0))
    mid_pre[...] = total
    mid = silu(total).astype(jnp.bfloat16)

    head_high = head[...].astype(jnp.bfloat16)
    head_low = (head[...] - head_high.astype(jnp.float32)).astype(jnp.bfloat16)
    spread = dot(head_high, mid) + dot(head_low, mid)
    for x in range(4):
        for y in range(6):
            block = None
            for cell in (0, 1):
                tap = y - 2 * cell
                if 0 <= tap < 4:
                    piece = spread[(4 * x + tap) * 32 : (4 * x + tap + 1) * 32,
                                   cell * 128 : cell * 128 + 128]
                    block = piece if block is None else block + piece
            partial[x, y, :, lanes(0)] = block[8:16] + earlier_cell(block[24:32])
            partial[x, y, :, lanes(1)] = block[16:24] + later_cell(block[0:8])
    copies = exchange(1, partial, arrived, spill_places)
    own_logits = []
    for column in range(8):
        own_logits.append(dot(heads, split[pl.ds(column * 128, 128), :])[:8])
    finish(copies, arrived)
    classes = lax.broadcasted_iota(jnp.int32, (8, 256), 0)
    for a in (0, 1):
        for y in range(4):
            x_at, y_at = 1 + a, 1 + y
            value = own_logits[4 * a + y] + partial[x_at, y_at]
            x_side = 0 if a == 0 else 3
            value = value + arrived[x_side, y_at]
            if y in (0, 3):
                y_side = 0 if y == 0 else 5
                value = value + arrived[x_at, y_side] + arrived[x_side, y_side]
            label = label_rows[4 * a + y : 4 * a + y + 1, :]
            target = (classes.astype(jnp.float32) == label).astype(jnp.float32)
            grad = jax.nn.sigmoid(value) - target
            grad = jnp.where(classes < 4, grad, 0.0)
            logit_grad[x_at, y_at] = grad.astype(jnp.bfloat16).astype(jnp.float32)
    copies = exchange(2, logit_grad, logit_grad, upper_places)
    slope = silu_slope(mid_pre[...])
    head_t_high = head_t[...].astype(jnp.bfloat16)
    head_t_low = (head_t[...] - head_t_high.astype(jnp.float32)).astype(jnp.bfloat16)
    finish(copies, logit_grad)
    for x in range(4):
        for y in range(6):
            even, odd = logit_grad[x, y, :, lanes(0)], logit_grad[x, y, :, lanes(1)]
            block = jnp.concatenate([earlier_cell(odd), even, odd, later_cell(even)], axis=0)
            block = block.astype(jnp.bfloat16)
            for cell in (0, 1):
                tap = y - 2 * cell
                if 0 <= tap < 4:
                    columns[pl.ds((4 * x + tap) * 32, 32), lanes(cell)] = block
    mid_grad = dot(head_t_high, columns[...]) + dot(head_t_low, columns[...])
    mid_pre_grad = (mid_grad * slope).astype(jnp.bfloat16)
    turned = jnp.transpose(mid_pre_grad)
    back[1, 1] = turned[:128]
    back[1, 2] = turned[128:]
    copies = exchange(3, back, back, brick_places)

    def keep(start, value):
        value = value.astype(jnp.bfloat16)
        rows = pl.ds(start, value.shape[0])
        part[0, rows] = value[:, :128]
        part[1, rows] = value[:, 128:]

    thirds = range(3)
    for tap in range(27):
        a, b, c = tap // 9, tap // 3 % 3, tap % 3
        cells = jnp.concatenate([low_moved[c, a, b], low_moved[c, a, b + 1]], axis=1)
        keep(tap * 256, dot(mid_pre_grad, cells, NT))
        if tap in (9, 19):
            summing.send_other(tap // 10)
    keep(27 * 256, dot(columns[...], mid, NT))
    keep(27 * 256 + 512, jnp.zeros((256, 256), jnp.float32))
    summing.send_other(2)
    for k in thirds:
        summing.add_other(k)
        summing.open_ring(k)
    for k in thirds:
        summing.pass_ring(k)

    finish(copies, back)
    rows, cols = grid_of(256, 128)
    moves = table(cols == jnp.where(rows < 128, rows + 1, rows - 129))
    for x in range(3):
        for y in range(4):
            back_moved[x, y, :, pl.ds(256, 256)] = back[x, y]
            both = dot(moves, back[x, y]).astype(jnp.bfloat16)
            back_moved[x, y, :, pl.ds(0, 256)] = both[:128]
            back_moved[x, y, :, pl.ds(512, 256)] = both[128:]
    for k in thirds:
        summing.store_sum(k, 0)
        summing.open_level(k, 1)

    total = jnp.zeros((256, 256), jnp.float32)
    for a in range(3):
        for b in range(3):
            cells = jnp.concatenate(
                [back_moved[2 - a, 2 - b], back_moved[2 - a, 3 - b]], axis=0
            )
            total = total + dot(cells, w_mid[pl.ds((3 * a + b) * 768, 768), :])
    down_grad = (jnp.transpose(total) * silu_slope(down_pre[...])).astype(jnp.bfloat16)
    for k in thirds:
        summing.store_sum(k, 1)
        summing.open_level(k, 2)

    def finish_features(a):
        for b in (0, 1):
            weight = jnp.concatenate([w_down[4 * a + 2 * b], w_down[4 * a + 2 * b + 1]], axis=1)
            pieces = dot(weight, down_grad, TN)
            for cell in (0, 1):
                y = 2 * cell + b
                grad = jnp.concatenate(
                    [logit_grad[1 + a, 1 + y], jnp.zeros((8, 256), jnp.float32)], axis=0
                ).astype(jnp.bfloat16)
                hidden = dot(heads, grad, TN).astype(jnp.bfloat16).astype(jnp.float32)
                at = slice(cell * 128, cell * 128 + 128)
                whole = jnp.concatenate([pieces[:128, at], pieces[128:, at]], axis=1) + hidden
                grad_out[pl.ds((4 * a + y) * 128, 128), :] = dot(
                    whole.astype(jnp.bfloat16), apart, NT
                ).astype(jnp.bfloat16)

    finish_features(0)
    for k in thirds:
        summing.store_last(k, scale)
        summing.open_spread(k, 2)
    finish_features(1)
    for k in thirds:
        summing.close_spread(k, 2)
        summing.open_spread(k, 1)
    for k in thirds:
        summing.close_spread(k, 1)
        summing.open_spread(k, 0)
    for k in thirds:
        summing.hand_own(k)
    for k in thirds:
        summing.pass_spread(k)
    for k in thirds:
        summing.hand_sides(k)
    for k in thirds:
        summing.hand_far(k)
    for copy in sent:
        copy.wait_send()
    summing.end()


def expand_kernel(sums, head_rows, mid_out, up_out, w_head, mixed, up, load_sem, mid_sem, up_sem):
    mid_copy = pltpu.make_async_copy(sums.at[pl.ds(0, 6912)], mid_out, mid_sem)
    load = pltpu.make_async_copy(sums.at[pl.ds(6912, 512)], mixed, load_sem)
    load.start()
    mid_copy.start()
    w_head[...] = jnp.zeros((16, 256), jnp.float32)
    w_head[pl.ds(0, 4), pl.ds(0, 128)] = head_rows[...].astype(jnp.float32)
    w_head[pl.ds(8, 4), pl.ds(128, 128)] = head_rows[...].astype(jnp.float32)
    heads = jnp.transpose(w_head[...]).astype(jnp.bfloat16)
    load.wait()
    stores = []
    for pair in range(32):
        pairs = dot(heads, mixed[pl.ds(pair * 16, 16), :])
        up[pl.ds(pair * 256, 256), :] = pairs.astype(jnp.bfloat16)
        if pair % 8 == 7:
            rows = pl.ds((pair - 7) * 256, 2048)
            store = pltpu.make_async_copy(up.at[rows], up_out.at[rows], up_sem.at[pair // 8])
            store.start()
            stores.append(store)
    for store in stores:
        store.wait()
    mid_copy.wait()


def expand(sums, w_head):
    vmem, hbm = pl.BlockSpec(memory_space=pltpu.VMEM), pl.BlockSpec(memory_space=pl.ANY)
    return pl.pallas_call(
        expand_kernel,
        out_shape=[
            jax.ShapeDtypeStruct((6912, 256), jnp.bfloat16),
            jax.ShapeDtypeStruct((8192, 256), jnp.bfloat16),
        ],
        in_specs=[hbm, vmem],
        out_specs=[hbm, hbm],
        scratch_shapes=[
            pltpu.VMEM((16, 256), jnp.float32),
            pltpu.VMEM((512, 256), jnp.bfloat16),
            pltpu.VMEM((8192, 256), jnp.bfloat16),
            pltpu.SemaphoreType.DMA(()),
            pltpu.SemaphoreType.DMA(()),
            pltpu.SemaphoreType.DMA((4,)),
        ],
        compiler_params=pltpu.CompilerParams(vmem_limit_bytes=32 * 2**20),
        cost_estimate=pl.CostEstimate(flops=10**8, bytes_accessed=12 * 10**6, transcendentals=0),
        name="expand",
    )(sums, w_head)


def window(features, labels, w_down, w_mid, w_up, w_head):
    half = lambda *shape: pltpu.VMEM(shape, jnp.bfloat16)
    full = lambda *shape: pltpu.VMEM(shape, jnp.float32)
    vmem, hbm = pl.BlockSpec(memory_space=pltpu.VMEM), pl.BlockSpec(memory_space=pl.ANY)
    return pl.pallas_call(
        functools.partial(window_kernel, 1.0 / math.sqrt(32768)),
        out_shape=[
            jax.ShapeDtypeStruct((1024, 256), jnp.bfloat16),
            jax.ShapeDtypeStruct((ROWS, 256), jnp.bfloat16),
        ],
        in_specs=[vmem, vmem, vmem, vmem, hbm, hbm],
        out_specs=[vmem, hbm],
        scratch_shapes=[
            full(16, 128), full(8, 256),
            half(27 * 256, 256), half(64 * 128, 256),
            half(3, 4, 256, 128), half(3, 3, 4, 256, 128),
            full(256, 256), full(256, 256),
            half(1024, 256), full(512, 256), full(256, 512),
            full(4, 6, 8, 256), full(4, 6, 8, 256), full(4, 6, 8, 256),
            half(512, 256), half(3, 4, 128, 256), half(3, 4, 128, 768),
            half(2, ROWS, 128), half(ROWS, 128), half(ROWS, 128),
            half(3, 2, 320, 128),
            half(3, 2, 640, 128), half(3, 3, 160, 128), half(3, 3, 48, 128),
            half(3 * 640, 128), half(3 * THIRD, 128), half(3 * THIRD, 128),
            half(ROWS, 128),
            pltpu.SemaphoreType.DMA((2,)),
            pltpu.SemaphoreType.DMA((32,)),
            pltpu.SemaphoreType.DMA((32,)),
            pltpu.SemaphoreType.DMA((100,)),
            pltpu.SemaphoreType.DMA((100,)),
        ],
        compiler_params=pltpu.CompilerParams(
            collective_id=8, has_side_effects=True, vmem_limit_bytes=56 * 2**20
        ),
        cost_estimate=pl.CostEstimate(flops=4 * 10**9, bytes_accessed=2 * 10**7, transcendentals=0),
        name="window",
    )(features, labels, w_down, w_head, w_mid, w_up)


def local(features, labels, w_down, w_mid, w_up, w_head):
    chans_up = features.shape[0]
    chans_mid = w_mid.shape[3]
    flat = features.transpose(1, 2, 0, 3).reshape(8 * chans_up, 256)
    grad, sums = window(
        flat, labels, w_down.reshape(8, chans_mid, chans_up),
        w_mid.reshape(27 * chans_mid, chans_mid), w_up.reshape(64 * chans_up, chans_mid), w_head,
    )
    feature_grad = grad.reshape(2, 4, chans_up, 256).transpose(2, 0, 1, 3)
    mid_out, up_out = expand(sums, w_head)
    return (
        feature_grad,
        mid_out.reshape(3, 3, 3, chans_mid, chans_mid),
        up_out.reshape(4, 4, 4, chans_up, chans_mid),
    )


def solution(mesh):
    return jax.shard_map(
        local,
        mesh=mesh,
        in_specs=(P(None, "gx", "gy", None), P("gx", "gy", None), P(), P(), P(), P()),
        out_specs=(P(None, "gx", "gy", None), P(), P()),
        check_vma=False,
    )
```

profile of v0, /device:TPU:1, one launch (start us, length us, event | category | flops | bytes accessed | tf_op | source)
XLA Modules:
  0.0 88.6 jit_solution(15458472520595490111)
XLA Ops:
  0.6 1.9 %copy.9 = bf16[2,4,128,256]{3,2,1,0:T(8,128)(2,1)} copy(bf16[2,4,128,256]{3,1,0,2:T(4,128)(2,1)} %bitcast.11) | data formatting | bytes 1048576 | tf_op jit(solution)/shard_map/transpose | solution.py:657
  2.6 0.0 copy-start.1
  2.6 78.5 %window.1 = (bf16[1024,256]{1,0:T(8,128)(2,1)}, bf16[7680,256]{1,0:T(8,128)(2,1)}) custom-call(bf16[1024,256]{1,0:T(8,128)(2,1)} %bitcast.14, s32[2,4,256]{2,1,0:T(4,128)} %labels.1, bf16[8,256,128]{2,1,0:T(8,128)(2,1)} %bitcast.19, bf16[4,128]{1,0:T(4,128)(2,1)} %head_rows.3, bf16[6912,256]{1,0:T(8,128)(2,1)} %bitcast.17, bf16[8192,256]{1,0:T(8,128)(2,1)} %bitcast.15), custom_call_target="tpu_custom_call" | custom-call | flops 4000000000 | bytes 20000000 | tf_op jit(solution)/shard_map/window/pallas_call | solution.py:619
  81.1 2.2 %copy.12 = bf16[2,4,128,256]{3,1,0,2:T(4,128)(2,1)} copy(bf16[2,4,128,256]{3,2,1,0:T(8,128)(2,1)} %bitcast.13) | data formatting | bytes 1048576 | tf_op jit(solution)/shard_map/reshape | solution.py:662
  83.3 0.0 copy-done.1
  83.3 0.0 copy-start
  83.3 2.1 %copy-done = bf16[7680,256]{1,0:T(8,128)(2,1)S(1)} copy-done((bf16[7680,256]{1,0:T(8,128)(2,1)S(1)}, bf16[7680,256]{1,0:T(8,128)(2,1)}, u32[]{:S(2)}) %copy-start) | copy-done | bytes 3932184
  85.4 3.2 %expand.1 = (bf16[6912,256]{1,0:T(8,128)(2,1)}, bf16[8192,256]{1,0:T(8,128)(2,1)}) custom-call(bf16[7680,256]{1,0:T(8,128)(2,1)S(1)} %copy-done, bf16[4,128]{1,0:T(4,128)(2,1)S(1)} %copy-done.1), custom_call_target="tpu_custom_call" | custom-call | flops 100000000 | bytes 12000000 | tf_op jit(solution)/shard_map/expand/pallas_call | solution.py:593
Async XLA Ops:
  2.6 80.8 %copy-start.1 = (bf16[4,128]{1,0:T(4,128)(2,1)S(1)}, bf16[4,128]{1,0:T(4,128)(2,1)}, u32[]{:S(2)}) copy-start(bf16[4,128]{1,0:T(4,128)(2,1)} %head_rows.3) | copy-start | bytes 3076
  83.3 2.1 %copy-start = (bf16[7680,256]{1,0:T(8,128)(2,1)S(1)}, bf16[7680,256]{1,0:T(8,128)(2,1)}, u32[]{:S(2)}) copy-start(bf16[7680,256]{1,0:T(8,128)(2,1)} %get-tuple-element.8.sums) | copy-start | bytes 11796484
where the time goes:
time: 88.9 us; the launch traced here: 88.6 us
  Pallas kernels  81.7 us (92%)
  local copies, waits for them, and re-layouts  6.3 us (7%)
    pallas_call x1, Pallas kernels, window(): pl.pallas_call(functools.partial(window_kernel, 1.0 / math.sqrt(32768)),...  78.5 us
    pallas_call x1, Pallas kernels, expand(): pl.pallas_call(expand_kernel, out_shape=[jax.ShapeDtypeStruct((6912, 256)...  3.18 us
    reshape x1, local copies, waits for them, and re-layouts, local(): feature_grad = grad.reshape(2, 4, chans_up, 256).transpose(2, 0, 1, 3)  2.24 us
    unnamed x4, local copies, waits for them, and re-layouts  2.12 us
    transpose x1, local copies, waits for them, and re-layouts, local(): flat = features.transpose(1, 2, 0, 3).reshape(8 * chans_up, 256)  1.94 us

commit v1 on v0

--- a/solution.py
+++ b/solution.py
@@ -13,7 +13,7 @@
 PART = ROWS // 3
 SIZES = [(640, 320), (160, 80), (48, 32)]
 THIRD = 4 * 48
-STEP = 80
+STEP = 320
 
 
 def my_place():
@@ -140,7 +140,7 @@
 
     def close_level(self, k, level, store):
         size = SIZES[level][0]
-        step = 48 if level == 2 else STEP
+        step = (STEP, 160, 48)[level]
         copies = self.opened[k, level]
         for copy in copies[2:] if level == 0 else copies:
             copy.wait_recv()
@@ -160,7 +160,7 @@
         pitch = PART // 4 if level == 0 else THIRD
 
         def store(start, total):
-            self.sums[level][rows_at(k * pitch + start, STEP)] = total.astype(jnp.bfloat16)
+            self.sums[level][rows_at(k * pitch + start, total.shape[0])] = total.astype(jnp.bfloat16)
 
         self.close_level(k, level, store)
         if level == 1:
@@ -186,16 +186,40 @@
         ref, base = self.spread_rows(k, level)
         rows = rows_at(base + self.spots(k, level)[0] * size, size)
         self.spread[k, level] = [
-            self.send(ref.at[rows], ref.at[rows], self.peer(k, level, d))
-            for d in ((1, 3) if level == 0 else (1, 2, 3))
+            self.send(ref.at[rows], ref.at[rows], self.peer(k, level, d)) for d in (1, 2, 3)
         ]
+
+    def piece_at(self, k, slab, distance):
+        index = self.spots(k, 1)[(4 - distance) % 4]
+        return index, rows_at(k * PART + slab * 640 + index * 160, 160)
+
+    def send_piece(self, k, distance):
+        if distance:
+            self.spread[k, 1][distance - 1].wait_recv()
+        _, rows = self.piece_at(k, self.spots(k, 0)[0], distance)
+        src = self.res.at[rows]
+        self.spread[k, 0, distance] = [
+            self.send(src, src, self.peer(k, 0, d)) for d in (1, 3)
+        ]
+
+    def pass_piece(self, k, distance):
+        copies = self.spread[k, 0, distance]
+        for copy in copies:
+            copy.wait_recv()
+        _, up, _, down = self.spots(k, 0)
+        index, _ = self.piece_at(k, 0, distance)
+        first = index < 2
+        _, rows = self.piece_at(k, jnp.where(first, down, up), distance)
+        src = self.res.at[rows]
+        copies.append(self.send(src, src, self.peer(k, 0, jnp.where(first, 1, 3))))
+        for slab in (down, up):
+            self.hand_out(k * PART + slab * 640 + index * 160, 160)
 
     def close_spread(self, k, level):
         for copy in self.spread[k, level]:
             copy.wait_recv()
-        if level == 2:
-            base = k * PART + self.spots(k, 0)[0] * 640 + self.spots(k, 1)[0] * 160
-            self.res[rows_at(base, 160)] = self.piece[pl.ds(k * THIRD, 160)]
+        _, rows = self.piece_at(k, self.spots(k, 0)[0], 0)
+        self.res[rows] = self.piece[pl.ds(k * THIRD, 160)]
 
     def hand_out(self, start, count):
         rows = rows_at(start, count)
@@ -210,26 +234,9 @@
     def hand_own(self, k):
         self.hand_out(k * PART + self.spots(k, 0)[0] * 640, 640)
 
-    def pass_spread(self, k):
-        size, cut = SIZES[0]
-        base = k * PART
-        _, up, far, down = self.spots(k, 0)
-        copies = self.spread[k, 0]
-        copies[0].wait_recv()
-        rows = rows_at(base + down * size, cut)
-        copies.append(self.send(self.res.at[rows], self.res.at[rows], self.peer(k, 0, 1)))
-        copies[1].wait_recv()
-        rows = rows_at(base + up * size + cut, cut)
-        copies.append(self.send(self.res.at[rows], self.res.at[rows], self.peer(k, 0, 3)))
-
-    def hand_sides(self, k):
-        _, up, _, down = self.spots(k, 0)
-        self.hand_out(k * PART + down * 640, 640)
-        self.hand_out(k * PART + up * 640, 640)
-
     def hand_far(self, k):
-        for copy in self.spread[k, 0][2:]:
-            copy.wait_recv()
+        for distance in range(4):
+            self.spread[k, 0, distance][2].wait_recv()
         self.hand_out(k * PART + self.spots(k, 0)[2] * 640, 640)
 
     def end(self):
@@ -280,9 +287,9 @@
     return jnp.where(lane == 0, 0.0, pltpu.roll(block, 1, 1))
 
 
-def window_kernel(scale, features, labels, w_down, head_rows, w_mid_hbm, w_up_hbm, grad_out, sum_out,
-                  w_head, label_cells, w_mid, w_up, low, low_moved, down_pre, mid_pre, split, head, head_t,
-                  partial, arrived, logit_grad, columns, back, back_moved,
+def window_kernel(scale, features_hbm, labels, w_down_hbm, head_rows, w_mid_hbm, w_up_hbm,
+                  grad_hbm, sum_out, features, w_down, grad_out, w_head, label_cells, w_mid, w_up, low, low_moved, down_pre, mid_pre, split, head, head_t,
+                  partial, arrived, known, logit_grad, columns, back, back_moved,
                   part, got, work, half, slab0, slab1, slab2, sum0, sum1, piece, res,
                   load_sem, send_sem, recv_sem, sum_send, sum_recv):
     gx, gy = lax.axis_index("gx"), lax.axis_index("gy")
@@ -291,11 +298,11 @@
         return (lax.rem(gx + (dx + 16), 16), lax.rem(gy + (dy + 8), 8))
 
     loads = [
-        pltpu.make_async_copy(w_mid_hbm, w_mid, load_sem.at[0]),
-        pltpu.make_async_copy(w_up_hbm, w_up, load_sem.at[1]),
+        pltpu.make_async_copy(src, dst, load_sem.at[index])
+        for index, (src, dst) in enumerate(
+            [(w_mid_hbm, w_mid), (w_up_hbm, w_up), (features_hbm, features), (w_down_hbm, w_down)]
+        )
     ]
-    for load in loads:
-        load.start()
     barrier = pltpu.get_barrier_semaphore()
     summing = Summing(
         part, sum_out, got, work, half, (slab0, slab1, slab2), (sum0, sum1), piece, res,
@@ -304,6 +311,8 @@
     peers = [near(dx, dy) for dx, dy in NEAR] + summing.peers()
     for peer in peers:
         pl.semaphore_signal(barrier, inc=1, device_id=peer, device_id_type=MESH)
+    for index in (2, 3, 1, 0):
+        loads[index].start()
     w_head[...] = jnp.zeros((16, 128), jnp.float32)
     w_head[pl.ds(0, 4), :] = head_rows[...].astype(jnp.float32)
     heads = w_head[...].astype(jnp.bfloat16)
@@ -312,12 +321,13 @@
 
     sent = []
 
-    def exchange(stage, src, dst, places):
+    def exchange(stage, src, dst, places, apart=False):
         copies = []
         for index, (dx, dy) in enumerate(NEAR):
             src_x, dst_x, src_y, dst_y = places(dx, dy)
             copy = pltpu.make_async_remote_copy(
-                src_ref=src.at[src_x, src_y], dst_ref=dst.at[dst_x, dst_y],
+                src_ref=src.at[src_x, src_y],
+                dst_ref=dst.at[index, dst_x, dst_y] if apart else dst.at[dst_x, dst_y],
                 send_sem=send_sem.at[8 * stage + index], recv_sem=recv_sem.at[8 * stage + index],
                 device_id=near(dx, dy), device_id_type=MESH,
             )
@@ -364,15 +374,26 @@
         return src_x, dst_x, src_y, dst_y
 
     def spill_places(dx, dy):
-        src_x = {0: pl.ds(1, 2), 1: one(3), -1: one(0)}[dx]
-        src_y = {0: pl.ds(1, 4), 1: one(5), -1: one(0)}[dy]
-        _, dst_x, _, dst_y = upper_places(dx, dy)
+        low_two, all_x, all_y = pl.ds(0, 2), pl.ds(0, 4), pl.ds(0, 6)
+        src_x = {0: all_x, 1: pl.ds(2, 2), -1: low_two}[dx]
+        dst_x = {0: all_x, 1: low_two, -1: pl.ds(2, 2)}[dx]
+        src_y = {0: all_y, 1: pl.ds(4, 2), -1: low_two}[dy]
+        dst_y = {0: all_y, 1: low_two, -1: pl.ds(4, 2)}[dy]
         return src_x, dst_x, src_y, dst_y
+
+    inside_x = {0: (gx > 0).astype(jnp.float32), 1: (gx < 15).astype(jnp.float32)}
+    inside_y = {0: (gy > 0).astype(jnp.float32), 1: (gy < 7).astype(jnp.float32)}
+
+    def inside(value, x, y):
+        value = value if x is None else value * inside_x[x]
+        return value if y is None else value * inside_y[y]
 
     lanes = lambda i: pl.ds(i * 128, 128)
     rows, cols = grid_of(256, 256)
     apart = table(rows == jnp.where(cols < 128, 2 * cols, 2 * cols - 255))
+    loads[2].wait()
     split[...] = dot(features[...], apart).astype(jnp.bfloat16)
+    loads[3].wait()
     total = jnp.zeros((256, 256), jnp.float32)
     for a in (0, 1):
         for b in (0, 1):
@@ -392,7 +413,15 @@
     pl.semaphore_wait(barrier, len(peers))
     copies = exchange(0, low, low, brick_places)
 
+    own_logits = [
+        dot(heads, split[pl.ds(column * 128, 128), :])[:8] for column in range(8)
+    ]
     label_rows = dot(label_cells[...].astype(jnp.bfloat16), apart)
+    for a in (0, 1):
+        for y in range(4):
+            known[1 + a, 1 + y] = own_logits[4 * a + y]
+            known[1 + a, 1 + y, pl.ds(4, 1), :] = label_rows[4 * a + y : 4 * a + y + 1, :]
+    known_copies = exchange(2, known, known, upper_places)
     loads[1].wait()
     for tap in range(64):
         mixed = dot(heads, w_up[pl.ds(tap * 128, 128), :])
@@ -436,34 +465,31 @@
                     block = piece if block is None else block + piece
             partial[x, y, :, lanes(0)] = block[8:16] + earlier_cell(block[24:32])
             partial[x, y, :, lanes(1)] = block[16:24] + later_cell(block[0:8])
-    copies = exchange(1, partial, arrived, spill_places)
-    own_logits = []
-    for column in range(8):
-        own_logits.append(dot(heads, split[pl.ds(column * 128, 128), :])[:8])
-    finish(copies, arrived)
-    classes = lax.broadcasted_iota(jnp.int32, (8, 256), 0)
-    for a in (0, 1):
-        for y in range(4):
-            x_at, y_at = 1 + a, 1 + y
-            value = own_logits[4 * a + y] + partial[x_at, y_at]
-            x_side = 0 if a == 0 else 3
-            value = value + arrived[x_side, y_at]
-            if y in (0, 3):
-                y_side = 0 if y == 0 else 5
-                value = value + arrived[x_at, y_side] + arrived[x_side, y_side]
-            label = label_rows[4 * a + y : 4 * a + y + 1, :]
-            target = (classes.astype(jnp.float32) == label).astype(jnp.float32)
-            grad = jax.nn.sigmoid(value) - target
-            grad = jnp.where(classes < 4, grad, 0.0)
-            logit_grad[x_at, y_at] = grad.astype(jnp.bfloat16).astype(jnp.float32)
-    copies = exchange(2, logit_grad, logit_grad, upper_places)
+    copies = exchange(1, partial, arrived, spill_places, True)
     slope = silu_slope(mid_pre[...])
     head_t_high = head_t[...].astype(jnp.bfloat16)
     head_t_low = (head_t[...] - head_t_high.astype(jnp.float32)).astype(jnp.bfloat16)
-    finish(copies, logit_grad)
+    classes = lax.broadcasted_iota(jnp.int32, (8, 256), 0)
+    for copy in known_copies + copies:
+        copy.wait_recv()
     for x in range(4):
         for y in range(6):
-            even, odd = logit_grad[x, y, :, lanes(0)], logit_grad[x, y, :, lanes(1)]
+            value = known[x, y] + partial[x, y]
+            side_x = 0 if x < 2 else 1
+            side_y = {0: 0, 1: 0, 4: 1, 5: 1}.get(y)
+            from_x, from_y = 1 - 2 * side_x, None if side_y is None else 1 - 2 * side_y
+            value = value + inside(arrived[NEAR.index((from_x, 0)), x, y], side_x, None)
+            if side_y is not None:
+                value = value + inside(arrived[NEAR.index((0, from_y)), x, y], None, side_y)
+                value = value + inside(
+                    arrived[NEAR.index((from_x, from_y)), x, y], side_x, side_y
+                )
+            target = (classes.astype(jnp.float32) == known[x, y, pl.ds(4, 1), :])
+            grad = jax.nn.sigmoid(value) - target.astype(jnp.float32)
+            grad = jnp.where(classes < 4, grad, 0.0).astype(jnp.bfloat16).astype(jnp.float32)
+            grad = inside(grad, {0: 0, 3: 1}.get(x), {0: 0, 5: 1}.get(y))
+            logit_grad[x, y] = grad
+            even, odd = grad[:, :128], grad[:, 128:]
             block = jnp.concatenate([earlier_cell(odd), even, odd, later_cell(even)], axis=0)
             block = block.astype(jnp.bfloat16)
             for cell in (0, 1):
@@ -475,7 +501,6 @@
     turned = jnp.transpose(mid_pre_grad)
     back[1, 1] = turned[:128]
     back[1, 2] = turned[128:]
-    copies = exchange(3, back, back, brick_places)
 
     def keep(start, value):
         value = value.astype(jnp.bfloat16)
@@ -499,6 +524,23 @@
     for k in thirds:
         summing.pass_ring(k)
 
+    for k in thirds:
+        summing.store_sum(k, 0)
+        summing.open_level(k, 1)
+
+    for k in thirds:
+        summing.store_sum(k, 1)
+        summing.open_level(k, 2)
+    copies = exchange(3, back, back, brick_places)
+
+    for k in thirds:
+        summing.store_last(k, scale)
+        summing.open_spread(k, 2)
+    for k in thirds:
+        summing.close_spread(k, 2)
+        summing.open_spread(k, 1)
+        summing.send_piece(k, 0)
+
     finish(copies, back)
     rows, cols = grid_of(256, 128)
     moves = table(cols == jnp.where(rows < 128, rows + 1, rows - 129))
@@ -508,10 +550,6 @@
             both = dot(moves, back[x, y]).astype(jnp.bfloat16)
             back_moved[x, y, :, pl.ds(0, 256)] = both[:128]
             back_moved[x, y, :, pl.ds(512, 256)] = both[128:]
-    for k in thirds:
-        summing.store_sum(k, 0)
-        summing.open_level(k, 1)
-
     total = jnp.zeros((256, 256), jnp.float32)
     for a in range(3):
         for b in range(3):
@@ -519,10 +557,12 @@
                 [back_moved[2 - a, 2 - b], back_moved[2 - a, 3 - b]], axis=0
             )
             total = total + dot(cells, w_mid[pl.ds((3 * a + b) * 768, 768), :])
+    for distance in (1, 3, 2):
+        for k in thirds:
+            summing.send_piece(k, distance)
+    for k in thirds:
+        summing.hand_own(k)
     down_grad = (jnp.transpose(total) * silu_slope(down_pre[...])).astype(jnp.bfloat16)
-    for k in thirds:
-        summing.store_sum(k, 1)
-        summing.open_level(k, 2)
 
     def finish_features(a):
         for b in (0, 1):
@@ -541,27 +581,18 @@
                 ).astype(jnp.bfloat16)
 
     finish_features(0)
-    for k in thirds:
-        summing.store_last(k, scale)
-        summing.open_spread(k, 2)
+    for distance in (0, 1, 3, 2):
+        for k in thirds:
+            summing.pass_piece(k, distance)
     finish_features(1)
-    for k in thirds:
-        summing.close_spread(k, 2)
-        summing.open_spread(k, 1)
-    for k in thirds:
-        summing.close_spread(k, 1)
-        summing.open_spread(k, 0)
-    for k in thirds:
-        summing.hand_own(k)
-    for k in thirds:
-        summing.pass_spread(k)
-    for k in thirds:
-        summing.hand_sides(k)
+    store_grad = pltpu.make_async_copy(grad_out, grad_hbm, load_sem.at[4])
+    store_grad.start()
     for k in thirds:
         summing.hand_far(k)
     for copy in sent:
         copy.wait_send()
     summing.end()
+    store_grad.wait()
 
 
 def expand_kernel(sums, head_rows, mid_out, up_out, w_head, mixed, up, load_sem, mid_sem, up_sem):
@@ -622,29 +653,30 @@
             jax.ShapeDtypeStruct((1024, 256), jnp.bfloat16),
             jax.ShapeDtypeStruct((ROWS, 256), jnp.bfloat16),
         ],
-        in_specs=[vmem, vmem, vmem, vmem, hbm, hbm],
-        out_specs=[vmem, hbm],
+        in_specs=[hbm, vmem, hbm, vmem, hbm, hbm],
+        out_specs=[hbm, hbm],
         scratch_shapes=[
+            half(1024, 256), half(8, 256, 128), half(1024, 256),
             full(16, 128), full(8, 256),
             half(27 * 256, 256), half(64 * 128, 256),
             half(3, 4, 256, 128), half(3, 3, 4, 256, 128),
             full(256, 256), full(256, 256),
             half(1024, 256), full(512, 256), full(256, 512),
-            full(4, 6, 8, 256), full(4, 6, 8, 256), full(4, 6, 8, 256),
+            full(4, 6, 8, 256), full(8, 4, 6, 8, 256), full(4, 6, 8, 256), full(4, 6, 8, 256),
             half(512, 256), half(3, 4, 128, 256), half(3, 4, 128, 768),
             half(2, ROWS, 128), half(ROWS, 128), half(ROWS, 128),
             half(3, 2, 320, 128),
             half(3, 2, 640, 128), half(3, 3, 160, 128), half(3, 3, 48, 128),
             half(3 * 640, 128), half(3 * THIRD, 128), half(3 * THIRD, 128),
             half(ROWS, 128),
-            pltpu.SemaphoreType.DMA((2,)),
+            pltpu.SemaphoreType.DMA((5,)),
             pltpu.SemaphoreType.DMA((32,)),
             pltpu.SemaphoreType.DMA((32,)),
-            pltpu.SemaphoreType.DMA((100,)),
-            pltpu.SemaphoreType.DMA((100,)),
+            pltpu.SemaphoreType.DMA((200,)),
+            pltpu.SemaphoreType.DMA((200,)),
         ],
         compiler_params=pltpu.CompilerParams(
-            collective_id=8, has_side_effects=True, vmem_limit_bytes=56 * 2**20
+            collective_id=8, has_side_effects=True, vmem_limit_bytes=60 * 2**20
         ),
         cost_estimate=pl.CostEstimate(flops=4 * 10**9, bytes_accessed=2 * 10**7, transcendentals=0),
         name="window",

time: 88.9 us -> 84.8 us (0.954)
  Pallas kernels: 81.7 us -> 77.4 us
    pallas_call x1, Pallas kernels: 78.5 us -> 74.2 us  [window(): pl.pallas_call(functools.partial(window_kernel, 1.0 / math.sqrt(32768)),...]
where the time goes in v1:
time: 84.8 us; the launch traced here: 84.5 us
  Pallas kernels  77.4 us (91%)
  local copies, waits for them, and re-layouts  6.3 us (7%)
    pallas_call x1, Pallas kernels, window(): pl.pallas_call(functools.partial(window_kernel, 1.0 / math.sqrt(32768)),...  74.2 us
    pallas_call x1, Pallas kernels, expand(): pl.pallas_call(expand_kernel, out_shape=[jax.ShapeDtypeStruct((6912, 256)...  3.18 us
    reshape x1, local copies, waits for them, and re-layouts, local(): feature_grad = grad.reshape(2, 4, chans_up, 256).transpose(2, 0, 1, 3)  2.24 us
    unnamed x4, local copies, waits for them, and re-layouts  2.12 us
    transpose x1, local copies, waits for them, and re-layouts, local(): flat = features.transpose(1, 2, 0, 3).reshape(8 * chans_up, 256)  1.94 us

profile of v1, /device:TPU:1, one launch (start us, length us, event | category | flops | bytes accessed | tf_op | source)
XLA Modules:
  0.0 84.5 jit_solution(10365525827138722587)
XLA Ops:
  0.6 1.9 %copy.9 = bf16[2,4,128,256]{3,2,1,0:T(8,128)(2,1)} copy(bf16[2,4,128,256]{3,1,0,2:T(4,128)(2,1)} %bitcast.11) | data formatting | bytes 1048576 | tf_op jit(solution)/shard_map/transpose | solution.py:689
  2.6 0.0 copy-start.1
  2.6 74.2 %window.1 = (bf16[1024,256]{1,0:T(8,128)(2,1)}, bf16[7680,256]{1,0:T(8,128)(2,1)}) custom-call(bf16[1024,256]{1,0:T(8,128)(2,1)} %bitcast.14, s32[2,4,256]{2,1,0:T(4,128)} %labels.1, bf16[8,256,128]{2,1,0:T(8,128)(2,1)} %bitcast.19, bf16[4,128]{1,0:T(4,128)(2,1)} %head_rows.3, bf16[6912,256]{1,0:T(8,128)(2,1)} %bitcast.17, bf16[8192,256]{1,0:T(8,128)(2,1)} %bitcast.15), custom_call_target="tpu_custom_call" | custom-call | flops 4000000000 | bytes 20000000 | tf_op jit(solution)/shard_map/window/pallas_call | solution.py:650
  76.8 2.2 %copy.12 = bf16[2,4,128,256]{3,1,0,2:T(4,128)(2,1)} copy(bf16[2,4,128,256]{3,2,1,0:T(8,128)(2,1)} %bitcast.13) | data formatting | bytes 1048576 | tf_op jit(solution)/shard_map/reshape | solution.py:694
  79.1 0.0 copy-done.1
  79.1 0.0 copy-start
  79.1 2.1 %copy-done = bf16[7680,256]{1,0:T(8,128)(2,1)S(1)} copy-done((bf16[7680,256]{1,0:T(8,128)(2,1)S(1)}, bf16[7680,256]{1,0:T(8,128)(2,1)}, u32[]{:S(2)}) %copy-start) | copy-done | bytes 3932184
  81.2 3.2 %expand.1 = (bf16[6912,256]{1,0:T(8,128)(2,1)}, bf16[8192,256]{1,0:T(8,128)(2,1)}) custom-call(bf16[7680,256]{1,0:T(8,128)(2,1)S(1)} %copy-done, bf16[4,128]{1,0:T(4,128)(2,1)S(1)} %copy-done.1), custom_call_target="tpu_custom_call" | custom-call | flops 100000000 | bytes 12000000 | tf_op jit(solution)/shard_map/expand/pallas_call | solution.py:624
Async XLA Ops:
  2.6 76.5 %copy-start.1 = (bf16[4,128]{1,0:T(4,128)(2,1)S(1)}, bf16[4,128]{1,0:T(4,128)(2,1)}, u32[]{:S(2)}) copy-start(bf16[4,128]{1,0:T(4,128)(2,1)} %head_rows.3) | copy-start | bytes 3076
  79.1 2.1 %copy-start = (bf16[7680,256]{1,0:T(8,128)(2,1)S(1)}, bf16[7680,256]{1,0:T(8,128)(2,1)}, u32[]{:S(2)}) copy-start(bf16[7680,256]{1,0:T(8,128)(2,1)} %get-tuple-element.8.sums) | copy-start | bytes 11796484

commit v2 on v1

--- a/solution.py
+++ b/solution.py
@@ -247,7 +247,7 @@
             far.wait_recv()
 
 
-NEAR = [(0, 1), (0, -1), (1, 0), (-1, 0), (1, 1), (1, -1), (-1, 1), (-1, -1)]
+NEAR = [(1, 0), (-1, 0), (1, 1), (-1, -1), (1, -1), (-1, 1), (0, 1), (0, -1)]
 NN = (((1,), (0,)), ((), ()))
 NT = (((1,), (1,)), ((), ()))
 TN = (((0,), (0,)), ((), ()))

time: 84.8 us -> 84.2 us (level)
  no operation moved by 1% of the time
where the time goes in v2:
time: 84.2 us; the launch traced here: 83.9 us
  Pallas kernels  76.8 us (91%)
  local copies, waits for them, and re-layouts  6.3 us (7%)
    pallas_call x1, Pallas kernels, window(): pl.pallas_call(functools.partial(window_kernel, 1.0 / math.sqrt(32768)),...  73.6 us
    pallas_call x1, Pallas kernels, expand(): pl.pallas_call(expand_kernel, out_shape=[jax.ShapeDtypeStruct((6912, 256)...  3.18 us
    reshape x1, local copies, waits for them, and re-layouts, local(): feature_grad = grad.reshape(2, 4, chans_up, 256).transpose(2, 0, 1, 3)  2.24 us
    unnamed x4, local copies, waits for them, and re-layouts  2.12 us
    transpose x1, local copies, waits for them, and re-layouts, local(): flat = features.transpose(1, 2, 0, 3).reshape(8 * chans_up, 256)  1.94 us

profile of v2, /device:TPU:1, one launch (start us, length us, event | category | flops | bytes accessed | tf_op | source)
XLA Modules:
  0.0 83.9 jit_solution(1132443199945778887)
XLA Ops:
  0.6 1.9 %copy.9 = bf16[2,4,128,256]{3,2,1,0:T(8,128)(2,1)} copy(bf16[2,4,128,256]{3,1,0,2:T(4,128)(2,1)} %bitcast.11) | data formatting | bytes 1048576 | tf_op jit(solution)/shard_map/transpose | solution.py:689
  2.6 0.0 copy-start.1
  2.6 73.6 %window.1 = (bf16[1024,256]{1,0:T(8,128)(2,1)}, bf16[7680,256]{1,0:T(8,128)(2,1)}) custom-call(bf16[1024,256]{1,0:T(8,128)(2,1)} %bitcast.14, s32[2,4,256]{2,1,0:T(4,128)} %labels.1, bf16[8,256,128]{2,1,0:T(8,128)(2,1)} %bitcast.19, bf16[4,128]{1,0:T(4,128)(2,1)} %head_rows.3, bf16[6912,256]{1,0:T(8,128)(2,1)} %bitcast.17, bf16[8192,256]{1,0:T(8,128)(2,1)} %bitcast.15), custom_call_target="tpu_custom_call" | custom-call | flops 4000000000 | bytes 20000000 | tf_op jit(solution)/shard_map/window/pallas_call | solution.py:650
  76.2 2.2 %copy.12 = bf16[2,4,128,256]{3,1,0,2:T(4,128)(2,1)} copy(bf16[2,4,128,256]{3,2,1,0:T(8,128)(2,1)} %bitcast.13) | data formatting | bytes 1048576 | tf_op jit(solution)/shard_map/reshape | solution.py:694
  78.4 0.0 copy-done.1
  78.4 0.0 copy-start
  78.4 2.1 %copy-done = bf16[7680,256]{1,0:T(8,128)(2,1)S(1)} copy-done((bf16[7680,256]{1,0:T(8,128)(2,1)S(1)}, bf16[7680,256]{1,0:T(8,128)(2,1)}, u32[]{:S(2)}) %copy-start) | copy-done | bytes 3932184
  80.5 3.2 %expand.1 = (bf16[6912,256]{1,0:T(8,128)(2,1)}, bf16[8192,256]{1,0:T(8,128)(2,1)}) custom-call(bf16[7680,256]{1,0:T(8,128)(2,1)S(1)} %copy-done, bf16[4,128]{1,0:T(4,128)(2,1)S(1)} %copy-done.1), custom_call_target="tpu_custom_call" | custom-call | flops 100000000 | bytes 12000000 | tf_op jit(solution)/shard_map/expand/pallas_call | solution.py:624
Async XLA Ops:
  2.6 75.8 %copy-start.1 = (bf16[4,128]{1,0:T(4,128)(2,1)S(1)}, bf16[4,128]{1,0:T(4,128)(2,1)}, u32[]{:S(2)}) copy-start(bf16[4,128]{1,0:T(4,128)(2,1)} %head_rows.3) | copy-start | bytes 3076
  78.4 2.1 %copy-start = (bf16[7680,256]{1,0:T(8,128)(2,1)S(1)}, bf16[7680,256]{1,0:T(8,128)(2,1)}, u32[]{:S(2)}) copy-start(bf16[7680,256]{1,0:T(8,128)(2,1)} %get-tuple-element.8.sums) | copy-start | bytes 11796484

commit v3 on v2

--- a/solution.py
+++ b/solution.py
@@ -97,36 +97,37 @@
         after, before = self.peer(k, 0, 1), self.peer(k, 0, 3)
         base = k * PART
         src, slab = self.work, self.slabs[0]
-        self.opened[k, 0] = [
-            self.send(src.at[rows_at(base + far * size, cut)], self.half.at[k, 0], after),
-            self.send(src.at[rows_at(base + far * size + cut, cut)], self.half.at[k, 1], before),
+        copies = []
+        for start in (0, 160):
+            for side, target in ((0, after), (1, before)):
+                rows = rows_at(base + far * size + side * cut + start, 160)
+                copies.append(
+                    self.send(src.at[rows], self.half.at[k, side, pl.ds(start, 160)], target)
+                )
+        copies += [
             self.send(src.at[rows_at(base + up * size + cut, cut)],
                       slab.at[k, 0, pl.ds(cut, cut)], after),
             self.send(src.at[rows_at(base + down * size, cut)], slab.at[k, 1, pl.ds(0, cut)],
                       before),
         ]
+        self.opened[k, 0] = copies
 
     def pass_ring(self, k):
         size, cut = SIZES[0]
         _, up, _, down = self.spots(k, 0)
         base = k * PART
         slab, copies = self.slabs[0], self.opened[k, 0]
-        for side, start, target, at in (
-            (0, base + up * size, self.peer(k, 0, 1), 0),
-            (1, base + down * size + cut, self.peer(k, 0, 3), cut),
-        ):
-            copies[side].wait_recv()
-
-            def body(offset):
-                rows = rows_at(start + offset, STEP)
-                passed = self.half[k, side, rows_at(offset, STEP)]
-                self.work[rows] = self.work[rows] + passed
-
-            for_rows(cut, STEP, body)
-            copies.append(
-                self.send(self.work.at[rows_at(start, cut)], slab.at[k, side, pl.ds(at, cut)],
-                          target)
-            )
+        for step in (0, 160):
+            for side, start, target, at in (
+                (0, base + up * size, self.peer(k, 0, 1), 0),
+                (1, base + down * size + cut, self.peer(k, 0, 3), cut),
+            ):
+                copies[step // 80 + side].wait_recv()
+                rows = rows_at(start + step, 160)
+                self.work[rows] = self.work[rows] + self.half[k, side, pl.ds(step, 160)]
+                copies.append(
+                    self.send(self.work.at[rows], slab.at[k, side, pl.ds(at + step, 160)], target)
+                )
 
     def open_level(self, k, level):
         size = SIZES[level][0]
@@ -142,7 +143,7 @@
         size = SIZES[level][0]
         step = (STEP, 160, 48)[level]
         copies = self.opened[k, level]
-        for copy in copies[2:] if level == 0 else copies:
+        for copy in copies[4:] if level == 0 else copies:
             copy.wait_recv()
         src, base = (self.work, k * PART) if level == 0 else (self.sums[level - 1], k * 4 * size)
         base = base + self.spots(k, level)[0] * size

time: 84.2 us -> 83.8 us (level)
  no operation moved by 1% of the time
where the time goes in v3:
time: 83.8 us; the launch traced here: 83.5 us
  Pallas kernels  76.4 us (91%)
  local copies, waits for them, and re-layouts  6.3 us (8%)
    pallas_call x1, Pallas kernels, window(): pl.pallas_call(functools.partial(window_kernel, 1.0 / math.sqrt(32768)),...  73.2 us
    pallas_call x1, Pallas kernels, expand(): pl.pallas_call(expand_kernel, out_shape=[jax.ShapeDtypeStruct((6912, 256)...  3.18 us
    reshape x1, local copies, waits for them, and re-layouts, local(): feature_grad = grad.reshape(2, 4, chans_up, 256).transpose(2, 0, 1, 3)  2.24 us
    unnamed x4, local copies, waits for them, and re-layouts  2.12 us
    transpose x1, local copies, waits for them, and re-layouts, local(): flat = features.transpose(1, 2, 0, 3).reshape(8 * chans_up, 256)  1.94 us

profile of v3, /device:TPU:1, one launch (start us, length us, event | category | flops | bytes accessed | tf_op | source)
XLA Modules:
  0.0 83.5 jit_solution(10302209837461819641)
XLA Ops:
  0.6 1.9 %copy.9 = bf16[2,4,128,256]{3,2,1,0:T(8,128)(2,1)} copy(bf16[2,4,128,256]{3,1,0,2:T(4,128)(2,1)} %bitcast.11) | data formatting | bytes 1048576 | tf_op jit(solution)/shard_map/transpose | solution.py:690
  2.6 0.0 copy-start.1
  2.6 73.2 %window.1 = (bf16[1024,256]{1,0:T(8,128)(2,1)}, bf16[7680,256]{1,0:T(8,128)(2,1)}) custom-call(bf16[1024,256]{1,0:T(8,128)(2,1)} %bitcast.14, s32[2,4,256]{2,1,0:T(4,128)} %labels.1, bf16[8,256,128]{2,1,0:T(8,128)(2,1)} %bitcast.19, bf16[4,128]{1,0:T(4,128)(2,1)} %head_rows.3, bf16[6912,256]{1,0:T(8,128)(2,1)} %bitcast.17, bf16[8192,256]{1,0:T(8,128)(2,1)} %bitcast.15), custom_call_target="tpu_custom_call" | custom-call | flops 4000000000 | bytes 20000000 | tf_op jit(solution)/shard_map/window/pallas_call | solution.py:651
  75.8 2.2 %copy.12 = bf16[2,4,128,256]{3,1,0,2:T(4,128)(2,1)} copy(bf16[2,4,128,256]{3,2,1,0:T(8,128)(2,1)} %bitcast.13) | data formatting | bytes 1048576 | tf_op jit(solution)/shard_map/reshape | solution.py:695
  78.0 0.0 copy-done.1
  78.0 0.0 copy-start
  78.0 2.1 %copy-done = bf16[7680,256]{1,0:T(8,128)(2,1)S(1)} copy-done((bf16[7680,256]{1,0:T(8,128)(2,1)S(1)}, bf16[7680,256]{1,0:T(8,128)(2,1)}, u32[]{:S(2)}) %copy-start) | copy-done | bytes 3932184
  80.2 3.2 %expand.1 = (bf16[6912,256]{1,0:T(8,128)(2,1)}, bf16[8192,256]{1,0:T(8,128)(2,1)}) custom-call(bf16[7680,256]{1,0:T(8,128)(2,1)S(1)} %copy-done, bf16[4,128]{1,0:T(4,128)(2,1)S(1)} %copy-done.1), custom_call_target="tpu_custom_call" | custom-call | flops 100000000 | bytes 12000000 | tf_op jit(solution)/shard_map/expand/pallas_call | solution.py:625
Async XLA Ops:
  2.6 75.5 %copy-start.1 = (bf16[4,128]{1,0:T(4,128)(2,1)S(1)}, bf16[4,128]{1,0:T(4,128)(2,1)}, u32[]{:S(2)}) copy-start(bf16[4,128]{1,0:T(4,128)(2,1)} %head_rows.3) | copy-start | bytes 3076
  78.0 2.1 %copy-start = (bf16[7680,256]{1,0:T(8,128)(2,1)S(1)}, bf16[7680,256]{1,0:T(8,128)(2,1)}, u32[]{:S(2)}) copy-start(bf16[7680,256]{1,0:T(8,128)(2,1)} %get-tuple-element.8.sums) | copy-start | bytes 11796484

commit v4 on v3

--- a/solution.py
+++ b/solution.py
@@ -562,6 +562,8 @@
         for k in thirds:
             summing.send_piece(k, distance)
     for k in thirds:
+        summing.pass_piece(k, 0)
+    for k in thirds:
         summing.hand_own(k)
     down_grad = (jnp.transpose(total) * silu_slope(down_pre[...])).astype(jnp.bfloat16)
 
@@ -581,8 +583,10 @@
                     whole.astype(jnp.bfloat16), apart, NT
                 ).astype(jnp.bfloat16)
 
+    for k in thirds:
+        summing.pass_piece(k, 1)
     finish_features(0)
-    for distance in (0, 1, 3, 2):
+    for distance in (3, 2):
         for k in thirds:
             summing.pass_piece(k, distance)
     finish_features(1)

time: 83.8 us -> 84.4 us (level)
  no operation moved by 1% of the time
where the time goes in v4:
time: 84.4 us; the launch traced here: 84.1 us
  Pallas kernels  77 us (91%)
  local copies, waits for them, and re-layouts  6.3 us (7%)
    pallas_call x1, Pallas kernels, window(): pl.pallas_call(functools.partial(window_kernel, 1.0 / math.sqrt(32768)),...  73.8 us
    pallas_call x1, Pallas kernels, expand(): pl.pallas_call(expand_kernel, out_shape=[jax.ShapeDtypeStruct((6912, 256)...  3.18 us
    reshape x1, local copies, waits for them, and re-layouts, local(): feature_grad = grad.reshape(2, 4, chans_up, 256).transpose(2, 0, 1, 3)  2.24 us
    unnamed x4, local copies, waits for them, and re-layouts  2.12 us
    transpose x1, local copies, waits for them, and re-layouts, local(): flat = features.transpose(1, 2, 0, 3).reshape(8 * chans_up, 256)  1.94 us

profile of v4, /device:TPU:1, one launch (start us, length us, event | category | flops | bytes accessed | tf_op | source)
XLA Modules:
  0.0 84.1 jit_solution(10505960495400399877)
XLA Ops:
  0.6 1.9 %copy.9 = bf16[2,4,128,256]{3,2,1,0:T(8,128)(2,1)} copy(bf16[2,4,128,256]{3,1,0,2:T(4,128)(2,1)} %bitcast.11) | data formatting | bytes 1048576 | tf_op jit(solution)/shard_map/transpose | solution.py:694
  2.6 0.0 copy-start.1
  2.6 73.8 %window.1 = (bf16[1024,256]{1,0:T(8,128)(2,1)}, bf16[7680,256]{1,0:T(8,128)(2,1)}) custom-call(bf16[1024,256]{1,0:T(8,128)(2,1)} %bitcast.14, s32[2,4,256]{2,1,0:T(4,128)} %labels.1, bf16[8,256,128]{2,1,0:T(8,128)(2,1)} %bitcast.19, bf16[4,128]{1,0:T(4,128)(2,1)} %head_rows.3, bf16[6912,256]{1,0:T(8,128)(2,1)} %bitcast.17, bf16[8192,256]{1,0:T(8,128)(2,1)} %bitcast.15), custom_call_target="tpu_custom_call" | custom-call | flops 4000000000 | bytes 20000000 | tf_op jit(solution)/shard_map/window/pallas_call | solution.py:655
  76.4 2.2 %copy.12 = bf16[2,4,128,256]{3,1,0,2:T(4,128)(2,1)} copy(bf16[2,4,128,256]{3,2,1,0:T(8,128)(2,1)} %bitcast.13) | data formatting | bytes 1048576 | tf_op jit(solution)/shard_map/reshape | solution.py:699
  78.6 0.0 copy-done.1
  78.6 0.0 copy-start
  78.6 2.1 %copy-done = bf16[7680,256]{1,0:T(8,128)(2,1)S(1)} copy-done((bf16[7680,256]{1,0:T(8,128)(2,1)S(1)}, bf16[7680,256]{1,0:T(8,128)(2,1)}, u32[]{:S(2)}) %copy-start) | copy-done | bytes 3932184
  80.7 3.2 %expand.1 = (bf16[6912,256]{1,0:T(8,128)(2,1)}, bf16[8192,256]{1,0:T(8,128)(2,1)}) custom-call(bf16[7680,256]{1,0:T(8,128)(2,1)S(1)} %copy-done, bf16[4,128]{1,0:T(4,128)(2,1)S(1)} %copy-done.1), custom_call_target="tpu_custom_call" | custom-call | flops 100000000 | bytes 12000000 | tf_op jit(solution)/shard_map/expand/pallas_call | solution.py:629
Async XLA Ops:
  2.6 76.1 %copy-start.1 = (bf16[4,128]{1,0:T(4,128)(2,1)S(1)}, bf16[4,128]{1,0:T(4,128)(2,1)}, u32[]{:S(2)}) copy-start(bf16[4,128]{1,0:T(4,128)(2,1)} %head_rows.3) | copy-start | bytes 3076
  78.6 2.1 %copy-start = (bf16[7680,256]{1,0:T(8,128)(2,1)S(1)}, bf16[7680,256]{1,0:T(8,128)(2,1)}, u32[]{:S(2)}) copy-start(bf16[7680,256]{1,0:T(8,128)(2,1)} %get-tuple-element.8.sums) | copy-start | bytes 11796484

commit v5 on v3

--- a/solution.py
+++ b/solution.py
@@ -78,12 +78,13 @@
         return moved(self.place, self.axes[k][level], distance)
 
     def send_other(self, k):
-        rows = pl.ds(k * PART, PART)
+        rows = pl.ds(k * (PART // 2), PART // 2)
         src = self.part.at[1 - self.core, rows]
         self.first[k] = self.send(src, self.got.at[rows], self.other)
 
     def add_other(self, k):
-        self.first[k].wait_recv()
+        self.first[2 * k].wait_recv()
+        self.first[2 * k + 1].wait_recv()
 
         def body(start):
             rows = rows_at(k * PART + start, STEP)
@@ -514,11 +515,11 @@
         a, b, c = tap // 9, tap // 3 % 3, tap % 3
         cells = jnp.concatenate([low_moved[c, a, b], low_moved[c, a, b + 1]], axis=1)
         keep(tap * 256, dot(mid_pre_grad, cells, NT))
-        if tap in (9, 19):
-            summing.send_other(tap // 10)
+        if tap % 5 == 4:
+            summing.send_other(tap // 5)
     keep(27 * 256, dot(columns[...], mid, NT))
     keep(27 * 256 + 512, jnp.zeros((256, 256), jnp.float32))
-    summing.send_other(2)
+    summing.send_other(5)
     for k in thirds:
         summing.add_other(k)
         summing.open_ring(k)

time: 83.8 us -> 83.8 us (level)
  no operation moved by 1% of the time
where the time goes in v5:
time: 83.8 us; the launch traced here: 83.5 us
  Pallas kernels  76.4 us (91%)
  local copies, waits for them, and re-layouts  6.3 us (8%)
    pallas_call x1, Pallas kernels, window(): pl.pallas_call(functools.partial(window_kernel, 1.0 / math.sqrt(32768)),...  73.3 us
    pallas_call x1, Pallas kernels, expand(): pl.pallas_call(expand_kernel, out_shape=[jax.ShapeDtypeStruct((6912, 256)...  3.18 us
    reshape x1, local copies, waits for them, and re-layouts, local(): feature_grad = grad.reshape(2, 4, chans_up, 256).transpose(2, 0, 1, 3)  2.24 us
    unnamed x4, local copies, waits for them, and re-layouts  2.12 us
    transpose x1, local copies, waits for them, and re-layouts, local(): flat = features.transpose(1, 2, 0, 3).reshape(8 * chans_up, 256)  1.94 us

profile of v5, /device:TPU:1, one launch (start us, length us, event | category | flops | bytes accessed | tf_op | source)
XLA Modules:
  0.0 83.5 jit_solution(3839371642515697408)
XLA Ops:
  0.6 1.9 %copy.9 = bf16[2,4,128,256]{3,2,1,0:T(8,128)(2,1)} copy(bf16[2,4,128,256]{3,1,0,2:T(4,128)(2,1)} %bitcast.11) | data formatting | bytes 1048576 | tf_op jit(solution)/shard_map/transpose | solution.py:691
  2.6 0.0 copy-start.1
  2.6 73.3 %window.1 = (bf16[1024,256]{1,0:T(8,128)(2,1)}, bf16[7680,256]{1,0:T(8,128)(2,1)}) custom-call(bf16[1024,256]{1,0:T(8,128)(2,1)} %bitcast.14, s32[2,4,256]{2,1,0:T(4,128)} %labels.1, bf16[8,256,128]{2,1,0:T(8,128)(2,1)} %bitcast.19, bf16[4,128]{1,0:T(4,128)(2,1)} %head_rows.3, bf16[6912,256]{1,0:T(8,128)(2,1)} %bitcast.17, bf16[8192,256]{1,0:T(8,128)(2,1)} %bitcast.15), custom_call_target="tpu_custom_call" | custom-call | flops 4000000000 | bytes 20000000 | tf_op jit(solution)/shard_map/window/pallas_call | solution.py:652
  75.8 2.2 %copy.12 = bf16[2,4,128,256]{3,1,0,2:T(4,128)(2,1)} copy(bf16[2,4,128,256]{3,2,1,0:T(8,128)(2,1)} %bitcast.13) | data formatting | bytes 1048576 | tf_op jit(solution)/shard_map/reshape | solution.py:696
  78.1 0.0 copy-done.1
  78.1 0.0 copy-start
  78.1 2.1 %copy-done = bf16[7680,256]{1,0:T(8,128)(2,1)S(1)} copy-done((bf16[7680,256]{1,0:T(8,128)(2,1)S(1)}, bf16[7680,256]{1,0:T(8,128)(2,1)}, u32[]{:S(2)}) %copy-start) | copy-done | bytes 3932184
  80.2 3.2 %expand.1 = (bf16[6912,256]{1,0:T(8,128)(2,1)}, bf16[8192,256]{1,0:T(8,128)(2,1)}) custom-call(bf16[7680,256]{1,0:T(8,128)(2,1)S(1)} %copy-done, bf16[4,128]{1,0:T(4,128)(2,1)S(1)} %copy-done.1), custom_call_target="tpu_custom_call" | custom-call | flops 100000000 | bytes 12000000 | tf_op jit(solution)/shard_map/expand/pallas_call | solution.py:626
Async XLA Ops:
  2.6 75.5 %copy-start.1 = (bf16[4,128]{1,0:T(4,128)(2,1)S(1)}, bf16[4,128]{1,0:T(4,128)(2,1)}, u32[]{:S(2)}) copy-start(bf16[4,128]{1,0:T(4,128)(2,1)} %head_rows.3) | copy-start | bytes 3076
  78.1 2.1 %copy-start = (bf16[7680,256]{1,0:T(8,128)(2,1)S(1)}, bf16[7680,256]{1,0:T(8,128)(2,1)}, u32[]{:S(2)}) copy-start(bf16[7680,256]{1,0:T(8,128)(2,1)} %get-tuple-element.8.sums) | copy-start | bytes 11796484
